TPU v7x, 256 devices: a whole 4x4x8 slice. The times are simulated.
256 devices in a mesh: dp: 64 (over z, x, core), tensor: 4 (over y).
Axes of the slice: x: 4, y: 4, z: 8, core: 2. Of those that a mesh axis runs over, the one named last changes fastest.
Arguments:
- tokens: bfloat16 [65536, 896], P('dp'), may hold values from -6 to 6
- hidden_grad: bfloat16 [65536, 2432], P('dp', 'tensor'), may hold values from -6 to 6
- gate_weight: bfloat16 [896, 2432], P(None, 'tensor'), may hold values from -0.1875 to 0.1875
- up_weight: bfloat16 [896, 2432], P(None, 'tensor'), may hold values from -0.1875 to 0.1875
- gate_error: bfloat16 [64, 896, 2432], P('dp', None, 'tensor'), may hold values from -2 to 2
- up_error: bfloat16 [64, 896, 2432], P('dp', None, 'tensor'), may hold values from -2 to 2
- gate_basis: float32 [32, 2432], P(None, 'tensor'), may hold values from -6 to 6
- up_basis: float32 [32, 2432], P(None, 'tensor'), may hold values from -6 to 6
Outputs:
- input_grad: bfloat16 [65536, 896], P(('dp', 'tensor'))
- gate_update: bfloat16 [896, 2432], P(None, 'tensor')
- up_update: bfloat16 [896, 2432], P(None, 'tensor')
- gate_error_next: bfloat16 [64, 896, 2432], P('dp', None, 'tensor')
- up_error_next: bfloat16 [64, 896, 2432], P('dp', None, 'tensor')
All inputs are finite; a program needn't handle non-finite values.
Results may differ from a plain program's by a relative error of at most 0.0053.
Values sent between devices are 32-bit elements; how exact they have to be, the bound alone decides.
A program may use at most 128 MiB of HBM per device.

v0:
```python
import math

import jax
import jax.numpy as jnp
from jax import lax
from jax.sharding import PartitionSpec as P

PRECISE = lax.Precision.HIGHEST


def contract(operand_left, operand_right, left_axis, right_axis, precise):
    return lax.dot_general(
        operand_left,
        operand_right,
        (((left_axis,), (right_axis,)), ((), ())),
        precision=PRECISE if precise else None,
        preferred_element_type=jnp.float32,
    )


def orthonormal(gram_matrix, factor_block):
    order = gram_matrix.shape[0]
    positions = jnp.arange(order)

    def factor_step(column, lower):
        select = (positions == column).astype(jnp.float32)
        row_now = jnp.dot(select, lower, precision=PRECISE)
        residue = jnp.dot(gram_matrix, select, precision=PRECISE) - jnp.dot(
            lower, row_now, precision=PRECISE
        )
        pivot = jnp.sqrt(jnp.dot(select, residue, precision=PRECISE))
        new_column = jnp.where(positions >= column, residue / pivot, 0.0)
        return lower + new_column[:, None] * select[None, :]

    lower = lax.fori_loop(0, order, factor_step, jnp.zeros((order, order), jnp.float32))

    def solve_step(row, solved):
        select = (positions == row).astype(jnp.float32)
        row_now = jnp.dot(select, lower, precision=PRECISE)
        pivot = jnp.dot(row_now, select, precision=PRECISE)
        target = jnp.dot(select, factor_block, precision=PRECISE) - jnp.dot(
            row_now, solved, precision=PRECISE
        )
        return solved + select[:, None] * (target / pivot)[None, :]

    return lax.fori_loop(0, order, solve_step, jnp.zeros(factor_block.shape, jnp.float32))


def on_device(
    tokens, hidden_grad, gate_weight, up_weight, gate_error, up_error, gate_basis, up_basis
):
    gate_act = jnp.dot(tokens, gate_weight, preferred_element_type=jnp.float32)
    up_act = jnp.dot(tokens, up_weight, preferred_element_type=jnp.float32)
    squash = jax.nn.sigmoid(gate_act)
    cotangent = hidden_grad.astype(jnp.float32)
    gate_delta = (cotangent * up_act * squash * (1.0 + gate_act * (1.0 - squash))).astype(
        jnp.bfloat16
    )
    up_delta = (cotangent * gate_act * squash).astype(jnp.bfloat16)
    input_grad = lax.psum_scatter(
        contract(gate_delta, gate_weight, 1, 1, False) + contract(up_delta, up_weight, 1, 1, False),
        "tensor",
        scatter_dimension=0,
        tiled=True,
    ).astype(jnp.bfloat16)
    grad_scale = 1.0 / math.sqrt(tokens.shape[0])
    gate_full = contract(tokens, gate_delta, 0, 0, False) * grad_scale + gate_error[0].astype(
        jnp.float32
    )
    up_full = contract(tokens, up_delta, 0, 0, False) * grad_scale + up_error[0].astype(jnp.float32)
    gate_factor, up_factor = lax.psum(
        (contract(gate_basis, gate_full, 1, 1, True), contract(up_basis, up_full, 1, 1, True)),
        "tensor",
    )
    gate_share, up_share = (
        lax.psum_scatter(gate_factor, "dp", scatter_dimension=1, tiled=True),
        lax.psum_scatter(up_factor, "dp", scatter_dimension=1, tiled=True),
    )
    gate_gram, up_gram = lax.psum(
        (contract(gate_share, gate_share, 1, 1, True), contract(up_share, up_share, 1, 1, True)),
        "dp",
    )
    gate_hat, up_hat = (
        lax.all_gather(orthonormal(gate_gram, gate_share), "dp", axis=1, tiled=True),
        lax.all_gather(orthonormal(up_gram, up_share), "dp", axis=1, tiled=True),
    )
    gate_coef, up_coef = lax.psum(
        (contract(gate_hat, gate_full, 1, 0, True), contract(up_hat, up_full, 1, 0, True)), "dp"
    )
    replicas = lax.axis_size("dp")
    gate_approx = contract(gate_hat, gate_coef, 0, 0, True)
    up_approx = contract(up_hat, up_coef, 0, 0, True)
    gate_next = (gate_full - gate_approx / replicas)[None].astype(jnp.bfloat16)
    up_next = (up_full - up_approx / replicas)[None].astype(jnp.bfloat16)
    return (
        input_grad,
        gate_approx.astype(jnp.bfloat16),
        up_approx.astype(jnp.bfloat16),
        gate_next,
        up_next,
    )


def solution(mesh):
    placed = (
        P("dp", None),
        P("dp", "tensor"),
        P(None, "tensor"),
        P(None, "tensor"),
        P("dp", None, "tensor"),
        P("dp", None, "tensor"),
        P(None, "tensor"),
        P(None, "tensor"),
    )
    return jax.shard_map(
        on_device,
        mesh=mesh,
        in_specs=placed,
        out_specs=(
            P(("dp", "tensor"), None),
            P(None, "tensor"),
            P(None, "tensor"),
            P("dp", None, "tensor"),
            P("dp", None, "tensor"),
        ),
        check_vma=False,
    )
```

profile of v0, /device:TPU:1, one launch (start us, length us, event | category | flops | bytes accessed | tf_op | source)
XLA Modules:
  0.0 987.2 jit_solution(9735060595840076450)
XLA Ops:
  8.1 1.4 copy-done
  9.5 2.8 fusion.75
  12.4 2.0 fusion.68
  14.4 1.6 convert_add_fusion
  16.1 1.5 convert_add_fusion.1
  17.6 1.4 copy-done.3
  19.0 2.0 convolution_bitcast_fusion.11
  20.9 2.0 convolution_bitcast_fusion.10
  23.0 4.9 fusion.76
  29.1 171.2 %all-reduce.11.cloned.1.call-done = (f32[32,896]{1,0:T(8,128)}, f32[32,896]{1,0:T(8,128)}) async-done(((f32[32,896]{1,0:T(8,128)}, f32[32,896]{1,0:T(8,128)}), (f32[32,896]{1,0:T(8,128)}, f32[32,896]{1,0:T(8,128)})) %all-reduce.11.cloned.1.call-update) | async-done | bytes 229392
  200.3 0.8 constant_dynamic-slice_fusion
  201.2 13.3 %all-reduce.5 = (f32[32,14]{1,0:T(8,128)S(1)}, f32[32,14]{1,0:T(8,128)S(1)}) all-reduce(f32[32,14]{1,0:T(8,128)S(1)} %get-tuple-element.520, f32[32,14]{1,0:T(8,128)S(1)} %get-tuple-element.519), channel_id=1, replica_groups=mesh['dp'=64,'tensor'=4] {'tensor'}, use_global_device_ids=true, to_apply=%region_1.0 | all-reduce | flops 896 | bytes 7168 | tf_op jit(solution)/shard_map/psum | solution.py:71
  215.0 244.5 %all-reduce.2 = (f32[32,32]{1,0:T(8,128)S(1)}, f32[32,32]{1,0:T(8,128)S(1)}) all-reduce(f32[32,32]{1,0:T(8,128)S(1)} %fusion.77, f32[32,32]{1,0:T(8,128)S(1)} %fusion.79), channel_id=1, replica_groups=mesh['dp'=64,'tensor'=4] {'dp'}, use_global_device_ids=true, to_apply=%region_3.0 | all-reduce | flops 2048 | bytes 16384 | tf_op jit(solution)/shard_map/psum | solution.py:79
  459.5 57.9 %while.60 = (s32[]{:T(128)}, f32[32,32]{1,0:T(8,128)S(1)}, f32[32,32]{1,0:T(8,128)S(1)}, s32[]{:T(128)}, s32[]{:T(128)}) while((s32[]{:T(128)}, f32[32,32]{1,0:T(8,128)S(1)}, f32[32,32]{1,0:T(8,128)S(1)}, s32[]{:T(128)}, s32[]{:T(128)}) %tuple.144), condition=%wide.region_5.0_spmd.clone.clone, body=%wide.region_4.0_spmd.clone.clone.sunk | while | flops 42338 | bytes 21877 | solution.py:35
  517.3 55.2 %while.58 = (s32[]{:T(128)}, f32[32,14]{0,1:T(8,128)S(1)}, f32[32,14]{0,1:T(8,128)S(1)}, f32[32,32]{1,0:T(8,128)S(1)}, s32[]{:T(128)}, /*index=5*/s32[]{:T(128)}) while((s32[]{:T(128)}, f32[32,14]{0,1:T(8,128)S(1)}, f32[32,14]{0,1:T(8,128)S(1)}, f32[32,32]{1,0:T(8,128)S(1)}, s32[]{:T(128)}, /*index=5*/s32[]{:T(128)}) %tuple.147), condition=%wide.region_7.8_spmd.clone, body=%wide.region_6.0_spmd.clone.sunk | while | flops 25086 | bytes 12108 | solution.py:46
  518.2 0.8 fusion.148
  519.9 0.8 fusion.148
  521.6 0.8 fusion.148
  523.4 0.8 fusion.148
  525.1 0.8 fusion.148
  526.8 0.8 fusion.148
  528.5 0.8 fusion.148
  530.3 0.8 fusion.148
  532.0 0.8 fusion.148
  533.7 0.8 fusion.148
  535.4 0.8 fusion.148
  537.2 0.8 fusion.148
  538.9 0.8 fusion.148
  540.6 0.8 fusion.148
  542.3 0.8 fusion.148
  544.1 0.8 fusion.148
  545.8 0.8 fusion.148
  547.5 0.8 fusion.148
  549.2 0.8 fusion.148
  550.9 0.8 fusion.148
  552.7 0.8 fusion.148
  554.4 0.8 fusion.148
  556.1 0.8 fusion.148
  557.8 0.8 fusion.148
  559.6 0.8 fusion.148
  564.7 0.8 fusion.148
  566.5 0.8 fusion.148
  572.5 52.7 %all-gather = f32[64,14,32]{2,1,0:T(8,128)S(1)} all-gather(f32[1,14,32]{2,1,0:T(8,128)S(1)} %bitcast.192), channel_id=1, replica_groups=mesh['dp'=64,'tensor'=4] {'dp'}, dimensions={0}, use_global_device_ids=true | all-gather | bytes 116480 | tf_op jit(solution)/shard_map/all_gather | solution.py:84
  625.2 4.6 fusion.78
  629.8 57.9 %while.61 = (s32[]{:T(128)}, f32[32,32]{1,0:T(8,128)S(1)}, f32[32,32]{1,0:T(8,128)S(1)}, s32[]{:T(128)}, s32[]{:T(128)}) while((s32[]{:T(128)}, f32[32,32]{1,0:T(8,128)S(1)}, f32[32,32]{1,0:T(8,128)S(1)}, s32[]{:T(128)}, s32[]{:T(128)}) %tuple.150), condition=%wide.region_13.14_spmd.clone.clone, body=%wide.region_12.13_spmd.clone.clone.sunk | while | flops 42338 | bytes 21877 | solution.py:35
  687.7 55.2 %while.59 = (s32[]{:T(128)}, f32[32,14]{0,1:T(8,128)S(1)}, f32[32,14]{0,1:T(8,128)S(1)}, f32[32,32]{1,0:T(8,128)S(1)}, s32[]{:T(128)}, /*index=5*/s32[]{:T(128)}) while((s32[]{:T(128)}, f32[32,14]{0,1:T(8,128)S(1)}, f32[32,14]{0,1:T(8,128)S(1)}, f32[32,32]{1,0:T(8,128)S(1)}, s32[]{:T(128)}, /*index=5*/s32[]{:T(128)}) %tuple.153), condition=%wide.region_15.16_spmd.clone, body=%wide.region_14.15_spmd.clone.sunk | while | flops 25086 | bytes 12108 | solution.py:46
  688.6 0.8 fusion.155
  695.5 0.8 fusion.155
  697.2 0.8 fusion.155
  704.1 0.8 fusion.155
  705.8 0.8 fusion.155
  712.7 0.8 fusion.155
  721.3 0.8 fusion.155
  728.2 0.8 fusion.155
  730.0 0.8 fusion.155
  736.8 0.8 fusion.155
  738.6 0.8 fusion.155
  742.9 50.0 %all-gather.1 = f32[64,14,32]{2,1,0:T(8,128)S(1)} all-gather(f32[1,14,32]{2,1,0:T(8,128)S(1)} %bitcast.191), channel_id=1, replica_groups=mesh['dp'=64,'tensor'=4] {'dp'}, dimensions={0}, use_global_device_ids=true | all-gather | bytes 116480 | tf_op jit(solution)/shard_map/all_gather | solution.py:85
  792.9 4.6 fusion.80
  797.8 7.2 convolution_add_fusion
  805.0 164.3 %all-reduce.9.cloned.1.call-done = (f32[32,608]{1,0:T(8,128)}, f32[32,608]{1,0:T(8,128)}) async-done(((f32[32,608]{1,0:T(8,128)}, f32[32,608]{1,0:T(8,128)}), (f32[32,608]{1,0:T(8,128)}, f32[32,608]{1,0:T(8,128)})) %all-reduce.9.cloned.1.call-update) | async-done | bytes 155664 | tf_op jit(solution)/shard_map/psum | solution.py:87
  969.3 5.1 fusion.71
  974.4 3.4 fusion.72
  977.8 2.0 convert_element_type.89
  (712 shorter events, 152.9 us)
Async XLA Ops:
  8.0 1.5 copy-start
  8.0 4.3 copy-start.7
  8.0 192.3 %all-reduce.11.cloned.1.call-start = ((), (), s32[]{:S(2)}) async-start(), calls=%async_computation.3 | async-start | bytes 458752
  9.5 2.8 copy-start.11
  12.3 2.0 copy-start.14
  12.3 2.0 copy-start.8
  14.4 1.6 copy-start.13
  14.4 1.7 copy-start.9
  16.1 4.8 copy-start.1
  16.1 2.9 copy-start.4
  17.6 1.4 copy-start.3
  19.0 2.0 copy-start.5
  19.0 4.0 copy-start.10
  22.9 5.0 copy-start.12
  23.0 946.3 %all-reduce.9.cloned.1.call-start = ((), (), s32[]{:S(2)}) async-start(), calls=%async_computation.2 | async-start | bytes 327680 | tf_op jit(solution)/shard_map/psum | solution.py:87
  797.5 180.2 %reduce-scatter.4.cloned.1.call-start = ((), (), s32[]{:S(2)}) async-start(), calls=%async_computation.1 | async-start | bytes 4587520 | tf_op jit(solution)/shard_map/reduce_scatter | solution.py:60
  969.3 5.1 copy-start.2
  969.3 5.1 copy-start.6
Sparse Core Ops, SparseCore 0:
  23.1 177.2 all-reduce.10
  797.7 171.5 all-reduce.8
Sparse Core Ops, SparseCore 1:
  805.1 39.2 reduce-scatter.3
where the time goes:
time: 989 us; the launch traced here: 987 us
  blocking collectives  361 us (37%)
  waiting for transfers between devices  336 us (34%)
  matrix products  212 us (21%)
  loops' own time  45.6 us (5%)
  between operations  16.3 us (2%)
  other arithmetic  12.5 us (1%)
    psum x1, blocking collectives, on_device(): lax.psum((contract(gate_share, gate_share, 1, 1, True), contract(up_share...  244 us
    unnamed x4, waiting for transfers between devices  171 us
    psum x1, waiting for transfers between devices, on_device(): lax.psum((contract(gate_hat, gate_full, 1, 0, True), contract(up_hat, up_...  164 us
    all_gather x1, blocking collectives, on_device(): lax.all_gather(orthonormal(gate_gram, gate_share), 'dp', axis=1, tiled=True)  52.7 us
    all_gather x1, blocking collectives, on_device(): lax.all_gather(orthonormal(up_gram, up_share), 'dp', axis=1, tiled=True)  50 us
    dot_general x64, matrix products, solve_step(): jnp.dot(row_now, solved, precision=PRECISE)  49.3 us
    dot_general x64, matrix products, factor_step(): jnp.dot(lower, row_now, precision=PRECISE)  49 us
    dot_general x64, matrix products, solve_step(): row_now = jnp.dot(select, lower, precision=PRECISE)  47.8 us
  transfers between devices with their start and end apart: 3, of which 2 were waited for; matrix products, arithmetic and copies ran while one was open for 2% of the time, Pallas kernels for 0%

commit v1 on v0

v1 whole, which is shorter than its diff:
```python
import functools
import math

import jax
import jax.numpy as jnp
from jax import lax
from jax.experimental import pallas as pl
from jax.experimental.pallas import tpu as pltpu
from jax.sharding import PartitionSpec as P

MESH = pl.DeviceIdType.MESH
F32 = jnp.float32
BF16 = jnp.bfloat16
HIGH = lax.Precision.HIGHEST
NZ, NX, NC, NY = 8, 4, 2, 4
D, FF, RANK, TOK = 896, 608, 32, 1024
ROWS = TOK // NY
HALF = ROWS // 2
SHARE = RANK // (NX * NY)
CROWS = RANK // NX
SCALE = 1.0 / math.sqrt(TOK)


def mm(a, b, ca, cb, precision=None):
    return lax.dot_general(
        a, b, (((ca,), (cb,)), ((), ())), precision=precision, preferred_element_type=F32
    )


def split_rows(a):
    high = a.astype(BF16)
    low = (a - high.astype(F32)).astype(BF16)
    return jnp.concatenate([high, low], axis=0)


def fold(a):
    return a[:RANK] + a[RANK:]


def device(z, x, c, y):
    return ((z * NX + x) * NC + c, y)


def main_kernel(
    tok_h, hid_h, wg_h, wu_h, eg_h, eu_h, bg_h, bu_h,
    ig_o, full_o, coef_o, stack_o,
    tok, hid, wgt, err, basis, delta, part, half_in, whole_in, ig_b,
    full, mate_full, s_high, s_low,
    f_out, f_in, f_src, f_rs, f_z, f_ag, fac, elim, h_own, h_all, stack,
    c_src, c_rs, c_z, c_all,
    in_sem, out_sem, send_sem, recv_sem,
):
    dp = lax.axis_index("dp")
    y = lax.axis_index("tensor")
    c = lax.rem(dp, NC)
    x = lax.rem(lax.div(dp, NC), NX)
    z = lax.div(dp, NC * NX)
    mate = 1 - c

    loads = [
        pltpu.make_async_copy(src, dst, in_sem.at[i])
        for i, (src, dst) in enumerate(
            [
                (wg_h, wgt.at[pl.ds(0, FF)]),
                (wu_h, wgt.at[pl.ds(FF, FF)]),
                (tok_h, tok),
                (hid_h, hid),
                (bg_h, basis.at[0]),
                (bu_h, basis.at[1]),
                (eg_h.at[0], err.at[0]),
                (eu_h.at[0], err.at[1]),
            ]
        )
    ]
    for load in loads:
        load.start()

    def at_xy(dx, dy):
        return device(z, lax.rem(x + dx, NX), c, lax.rem(y + dy, NY))

    def at_z(dz):
        return device(lax.rem(z + dz, NZ), x, c, y)

    def at_cx(dc, dx):
        return device(z, lax.rem(x + dx, NX), lax.rem(c + dc, NC), y)

    xy = [(dx, dy) for dx in range(NX) for dy in range(NY)][1:]
    cx = [(dc, dx) for dc in range(NC) for dx in range(NX)][1:]
    greet = [at_xy(*o) for o in xy] + [at_z(dz) for dz in range(1, NZ)]
    greet += [at_cx(*o) for o in cx if o[0] == 1]
    barrier = pltpu.get_barrier_semaphore()
    for other in greet:
        pl.semaphore_signal(barrier, inc=1, device_id=other, device_id_type=MESH)

    used = [0]
    sent = []

    def send(src, dst, to):
        i = used[0]
        used[0] += 1
        copy = pltpu.make_async_remote_copy(
            src_ref=src, dst_ref=dst, send_sem=send_sem.at[i], recv_sem=recv_sem.at[i],
            device_id=to, device_id_type=MESH,
        )
        copy.start()
        sent.append(copy)
        return copy

    for load in loads[:4]:
        load.wait()

    def act_step(i, carry):
        cols = pl.ds(pl.multiple_of(i * ROWS, ROWS), ROWS)
        act = mm(wgt[...], tok[cols, :], 1, 1)
        g, u = act[:FF], act[FF:]
        h = hid[:, cols].astype(F32)
        s = 1.0 / (1.0 + jnp.exp(-g))
        hs = h * s
        delta[:FF, cols] = (hs * u * (1.0 + g * (1.0 - s))).astype(BF16)
        delta[FF:, cols] = (hs * g).astype(BF16)
        return carry

    with jax.named_scope("acts"):
        lax.fori_loop(0, NY, act_step, 0)
    for load in loads[4:]:
        load.wait()

    def pick(p):
        return pl.ds(pl.multiple_of(p * FF, FF), FF)

    def factor_of(p):
        b = split_rows(basis[p])
        t = fold(mm(b, delta[pick(p), :], 1, 0))
        e = fold(mm(b, err[p], 1, 0))
        return fold(mm(split_rows(t), tok[...], 1, 0)) * SCALE + e

    f_out[...] = factor_of(mate)
    pl.semaphore_wait(barrier, len(greet))
    ex_f = send(f_out, f_in, at_cx(1, 0))
    own = factor_of(c)
    ex_f.wait_recv()
    own = own + f_in[...]
    for s in range(NX * NY):
        f_src[s] = own[s * SHARE:(s + 1) * SHARE]
    rs = []
    for i, (dx, dy) in enumerate(xy):
        to = lax.rem(x + dx, NX) * NY + lax.rem(y + dy, NY)
        rs.append(send(f_src.at[to], f_rs.at[i], at_xy(dx, dy)))

    def partial(k):
        cols = pl.ds(pl.multiple_of(lax.rem(y + k, NY) * ROWS, ROWS), ROWS)
        part[k] = mm(delta[:, cols], wgt[...], 0, 0)

    low, high = pl.ds(0, HALF), pl.ds(HALF, HALF)
    partial(2)
    far_up = send(part.at[2, low], half_in.at[0], at_xy(0, 1))
    far_down = send(part.at[2, high], half_in.at[1], at_xy(0, NY - 1))
    partial(1)
    partial(3)

    mine = x * NY + y
    total = f_src[mine]
    for copy in rs:
        copy.wait_recv()
    for i in range(len(xy)):
        total = total + f_rs[i]
    f_z[z] = total
    zs = [send(f_z.at[z], f_z.at[z], at_z(dz)) for dz in range(1, NZ)]

    def grad_of(p):
        full[p] = mm(delta[pick(p), :], tok[...], 1, 0) * SCALE + err[p].astype(F32)

    grad_of(mate)
    ex_s = send(full.at[mate], mate_full, at_cx(1, 0))
    grad_of(c)

    for copy in zs:
        copy.wait_recv()
    total = f_z[0]
    for i in range(1, NZ):
        total = total + f_z[i]
    f_ag[mine] = total
    ag = [send(f_ag.at[mine], f_ag.at[mine], at_xy(dx, dy)) for dx, dy in xy]

    near_up = [send(part.at[1, high], whole_in.at[0, high], at_xy(0, 1))]
    near_down = [send(part.at[3, low], whole_in.at[1, low], at_xy(0, NY - 1))]
    far_up.wait_recv()
    part[1, low] = part[1, low] + half_in[0]
    near_up.append(send(part.at[1, low], whole_in.at[0, low], at_xy(0, 1)))
    far_down.wait_recv()
    part[3, high] = part[3, high] + half_in[1]
    near_down.append(send(part.at[3, high], whole_in.at[1, high], at_xy(0, NY - 1)))

    stores = [
        pltpu.make_async_copy(full, full_o, out_sem.at[0]),
        pltpu.make_async_copy(ig_b, ig_o, out_sem.at[1]),
        pltpu.make_async_copy(c_all, coef_o, out_sem.at[2]),
        pltpu.make_async_copy(stack, stack_o, out_sem.at[3]),
    ]
    stores[0].start()
    ex_s.wait_recv()
    both = (full[c] + mate_full[...]).T
    top = both.astype(BF16)
    s_high[...] = top
    s_low[...] = (both - top.astype(F32)).astype(BF16)
    partial(0)

    for copy in ag:
        copy.wait_recv()
    for s in range(NX * NY):
        fac[s * SHARE:(s + 1) * SHARE] = f_ag[s]
    factor = fac[...]
    pair = split_rows(factor)
    coef = fold(mm(pair, s_high[...], 1, 0)) + mm(pair[:RANK], s_low[...], 1, 0)
    for j in range(NX):
        c_src[j] = coef[j * CROWS:(j + 1) * CROWS]
    crs = [
        send(c_src.at[lax.rem(x + dx, NX)], c_rs.at[x], at_cx(0, dx)) for dx in range(1, NX)
    ]
    c_rs[x] = c_src[x]

    sub = lax.broadcasted_iota(jnp.int32, (RANK, 2 * RANK), 0)
    lane = lax.broadcasted_iota(jnp.int32, (RANK, 2 * RANK), 1)
    gram = mm(factor, factor, 1, 1, HIGH)
    elim[:, :RANK] = gram
    elim[:, RANK:] = (sub[:, :RANK] == lane[:, :RANK]).astype(F32)

    def eliminate(k, a):
        row = jnp.sum(jnp.where(sub == k, a, 0.0), axis=0, keepdims=True)
        column = jnp.sum(jnp.where(lane == k, a, 0.0), axis=1, keepdims=True)
        pivot = jnp.sum(jnp.where(lane[:1] == k, row, 0.0), axis=1, keepdims=True)
        return a - jnp.where(sub > k, (column / pivot) * row, 0.0)

    state = lax.fori_loop(0, RANK // 2, eliminate, elim[...])
    for copy in crs:
        copy.wait_recv()
    total = c_rs[0]
    for i in range(1, NX):
        total = total + c_rs[i]
    c_z[z] = total
    czs = [send(c_z.at[z], c_z.at[z], at_z(dz)) for dz in range(1, NZ)]

    state = lax.fori_loop(RANK // 2, RANK, eliminate, state)
    left, inverse = state[:, :RANK], state[:, RANK:]
    pivots = jnp.sum(
        jnp.where(sub[:, :RANK] == lane[:, :RANK], left, 0.0), axis=1, keepdims=True
    )
    inverse = inverse * lax.rsqrt(pivots)
    hat = mm(inverse, factor, 1, 0, HIGH)
    h_own[...] = mm(inverse, hat, 0, 0, HIGH)
    ex_h = send(h_own, h_all, at_cx(1, 0))

    for copy in czs:
        copy.wait_recv()
    total = c_z[0]
    for i in range(1, NZ):
        total = total + c_z[i]
    c_all[c, x] = total
    cag = [send(c_all.at[c, x], c_all.at[c, x], at_cx(dc, dx)) for dc, dx in cx]

    ex_h.wait_recv()
    for p, value in ((c, h_own[...]), (mate, h_all[...])):
        top = value.astype(BF16)
        stack[p, :RANK] = top
        stack[p, RANK:2 * RANK] = top
        stack[p, 2 * RANK:] = (value - top.astype(F32)).astype(BF16)
    stores[3].start()

    for copy in near_up + near_down:
        copy.wait_recv()
    ig_b[...] = (part[0] + (whole_in[0] + whole_in[1])).astype(BF16)
    stores[1].start()
    for copy in cag:
        copy.wait_recv()
    stores[2].start()
    for copy in sent:
        copy.wait_send()
    for store in stores:
        store.wait()


def final_kernel(ig, full, coef, stack, ig_o, gu_o, uu_o, ge_o, ue_o):
    @pl.when(pl.program_id(0) == 0)
    def _():
        ig_o[...] = ig[...]

    for p, (update, error) in enumerate(((gu_o, ge_o), (uu_o, ue_o))):
        value = coef[p]
        top = value.astype(BF16)
        low = (value - top.astype(F32)).astype(BF16)
        approx = mm(jnp.concatenate([top, low, top], axis=0), stack[p], 0, 0)
        update[...] = approx.astype(BF16)
        error[0] = (full[p] - approx * (1.0 / (NZ * NX * NC))).astype(BF16)


def on_device(tokens, hidden_grad, gate_weight, up_weight, gate_error, up_error, gate_basis, up_basis):
    V, S = pltpu.VMEM, pltpu.SemaphoreType.DMA
    any_spec = pl.BlockSpec(memory_space=pl.ANY)
    copies = 80
    ig, full, coef, stack = pl.pallas_call(
        main_kernel,
        name="main",
        out_shape=(
            jax.ShapeDtypeStruct((ROWS, D), BF16),
            jax.ShapeDtypeStruct((2, FF, D), F32),
            jax.ShapeDtypeStruct((2, NX, CROWS, FF), F32),
            jax.ShapeDtypeStruct((2, 3 * RANK, D), BF16),
        ),
        in_specs=[any_spec] * 8,
        out_specs=(any_spec,) * 4,
        scratch_shapes=[
            V((TOK, D), BF16), V((FF, TOK), BF16), V((2 * FF, D), BF16),
            V((2, FF, D), BF16), V((2, RANK, FF), F32), V((2 * FF, TOK), BF16),
            V((NY, ROWS, D), F32), V((2, HALF, D), F32), V((2, ROWS, D), F32), V((ROWS, D), BF16),
            V((2, FF, D), F32), V((FF, D), F32), V((D, FF), BF16), V((D, FF), BF16),
            V((RANK, D), F32), V((RANK, D), F32), V((NX * NY, SHARE, D), F32),
            V((NX * NY - 1, SHARE, D), F32), V((NZ, SHARE, D), F32), V((NX * NY, SHARE, D), F32),
            V((RANK, D), F32), V((RANK, 2 * RANK), F32), V((RANK, D), F32), V((RANK, D), F32),
            V((2, 3 * RANK, D), BF16),
            V((NX, CROWS, FF), F32), V((NX, CROWS, FF), F32), V((NZ, CROWS, FF), F32),
            V((2, NX, CROWS, FF), F32),
            S((8,)), S((4,)), S((copies,)), S((copies,)),
        ],
        compiler_params=pltpu.CompilerParams(
            collective_id=0, has_side_effects=True, vmem_limit_bytes=56 << 20
        ),
        cost_estimate=pl.CostEstimate(
            flops=8 * TOK * D * FF, bytes_accessed=16 << 20, transcendentals=TOK * FF
        ),
    )(
        tokens, hidden_grad.T, gate_weight.T, up_weight.T,
        jnp.swapaxes(gate_error, 1, 2), jnp.swapaxes(up_error, 1, 2), gate_basis, up_basis,
    )
    block = 128
    out = jax.ShapeDtypeStruct((FF, D), BF16)
    out_error = jax.ShapeDtypeStruct((1, FF, D), BF16)
    rows = pl.BlockSpec((block, D), lambda i: (i, 0))
    rows_error = pl.BlockSpec((1, block, D), lambda i: (0, i, 0))
    whole = pl.BlockSpec((ROWS, D), lambda i: (0, 0))
    input_grad, gate_update, up_update, gate_next, up_next = pl.pallas_call(
        final_kernel,
        name="outputs",
        grid=(pl.cdiv(FF, block),),
        out_shape=(jax.ShapeDtypeStruct((ROWS, D), BF16), out, out, out_error, out_error),
        in_specs=[
            whole,
            pl.BlockSpec((2, block, D), lambda i: (0, i, 0)),
            pl.BlockSpec((2, RANK, block), lambda i: (0, 0, i)),
            pl.BlockSpec((2, 3 * RANK, D), lambda i: (0, 0, 0)),
        ],
        out_specs=(whole, rows, rows, rows_error, rows_error),
        compiler_params=pltpu.CompilerParams(vmem_limit_bytes=56 << 20),
    )(ig, full, coef.reshape(2, RANK, FF), stack)
    return (
        input_grad, gate_update.T, up_update.T,
        jnp.swapaxes(gate_next, 1, 2), jnp.swapaxes(up_next, 1, 2),
    )


def solution(mesh):
    placed = (
        P("dp", None),
        P("dp", "tensor"),
        P(None, "tensor"),
        P(None, "tensor"),
        P("dp", None, "tensor"),
        P("dp", None, "tensor"),
        P(None, "tensor"),
        P(None, "tensor"),
    )
    return jax.shard_map(
        on_device,
        mesh=mesh,
        in_specs=placed,
        out_specs=(
            P(("dp", "tensor"), None),
            P(None, "tensor"),
            P(None, "tensor"),
            P("dp", None, "tensor"),
            P("dp", None, "tensor"),
        ),
        check_vma=False,
    )
```

time: 989 us -> 56.1 us (0.06)
  blocking collectives: 361 us -> 0 us
  waiting for transfers between devices: 336 us -> 0 us
  matrix products: 212 us -> 0 us
  Pallas kernels: 0 us -> 55.2 us
  loops' own time: 45.6 us -> 0 us
  between operations: 16.3 us -> 0.64 us
  other arithmetic: 12.5 us -> 0 us
    psum x2 -> x0, blocking collectives: 258 us -> none  [the longest x1 244 us: on_device(): lax.psum((contract(gate_share, gate_share, 1, 1, True), contract(up_share...]
    dot_general x398 -> x0, matrix products: 212 us -> none  [the longest x64 49.3 us: solve_step(): jnp.dot(row_now, solved, precision=PRECISE)]
    unnamed x4 -> x0, waiting for transfers between devices: 171 us -> none
    psum x1 -> x0, waiting for transfers between devices: 164 us -> none  [on_device(): lax.psum((contract(gate_hat, gate_full, 1, 0, True), contract(up_hat, up_...]
    all_gather x2 -> x0, blocking collectives: 103 us -> none  [the longest x1 52.7 us: on_device(): lax.all_gather(orthonormal(gate_gram, gate_share), 'dp', axis=1, tiled=True)]
    pallas_call x0 -> x2, Pallas kernels: none -> 55.2 us  [the longest x1 48.4 us: on_device(): pl.pallas_call(main_kernel, name='main', out_shape=(jax.ShapeDtypeStruct(...]
    another operation x4 -> x0, loops' own time: 45.6 us -> none  [the longest x2 45 us: orthonormal(): lax.fori_loop(0, order, factor_step, jnp.zeros((order, order), jnp.float32))]
  transfers between devices with their start and end apart: 3 -> 0, of which waited for: 2 -> 0; matrix products, arithmetic and copies ran while one was open for 2% -> 0% of each run, Pallas kernels for 0% -> 0%
where the time goes in v1:
time: 56.1 us; the launch traced here: 55.9 us
  Pallas kernels  55.2 us (98%)
  between operations  0.64 us (1%)
    pallas_call x1, Pallas kernels, on_device(): pl.pallas_call(main_kernel, name='main', out_shape=(jax.ShapeDtypeStruct(...  48.4 us
    pallas_call x1, Pallas kernels, on_device(): pl.pallas_call(final_kernel, name='outputs', grid=(pl.cdiv(FF, block),),...  6.79 us

profile of v1, /device:TPU:1, one launch (start us, length us, event | category | flops | bytes accessed | tf_op | source)
XLA Modules:
  0.0 55.9 jit_solution(3230697933159134346)
XLA Ops:
  0.6 48.4 %main.1 = (bf16[256,896]{1,0:T(8,128)(2,1)}, f32[2,608,896]{2,1,0:T(8,128)}, f32[2,4,8,608]{3,2,1,0:T(8,128)}, bf16[2,96,896]{2,1,0:T(8,128)(2,1)}) custom-call(bf16[1024,896]{1,0:T(8,128)(2,1)} %tok_h.1, bf16[608,1024]{1,0:T(8,128)(2,1)} %bitcast.11, bf16[608,896]{1,0:T(8,128)(2,1)} %bitcast.12, bf16[608,896]{1,0:T(8,128)(2,1)} %bitcast.13, ...), custom_call_target="tpu_custom_call" | custom-call | flops 4462739456 | bytes 16777216 | tf_op jit(solution)/shard_map/main/pallas_call | solution.py:300
  49.1 6.8 %outputs.1 = (bf16[256,896]{1,0:T(8,128)(2,1)}, bf16[608,896]{1,0:T(8,128)(2,1)}, bf16[608,896]{1,0:T(8,128)(2,1)}, bf16[1,608,896]{2,1,0:T(8,128)(2,1)}, bf16[1,608,896]{2,1,0:T(8,128)(2,1)}) custom-call(bf16[256,896]{1,0:T(8,128)(2,1)} %get-tuple-element.14.ig, f32[2,608,896]{2,1,0:T(8,128)} %get-tuple-element.15.full, f32[2,32,608]{2,1,0:T(8,128)} %bitcast.10, ...), custom_call_target="tpu_custom_call" | custom-call | tf_op jit(solution)/shard_map/outputs/pallas_call | solution.py:340

commit v2 on v1

--- a/solution.py
+++ b/solution.py
@@ -19,6 +19,7 @@
 SHARE = RANK // (NX * NY)
 CROWS = RANK // NX
 SCALE = 1.0 / math.sqrt(TOK)
+BLOCKS = ((0, 160), (160, 160), (320, 160), (480, 128))
 
 
 def mm(a, b, ca, cb, precision=None):
@@ -279,18 +280,29 @@
         store.wait()
 
 
-def final_kernel(ig, full, coef, stack, ig_o, gu_o, uu_o, ge_o, ue_o):
-    @pl.when(pl.program_id(0) == 0)
-    def _():
-        ig_o[...] = ig[...]
-
-    for p, (update, error) in enumerate(((gu_o, ge_o), (uu_o, ue_o))):
+def final_kernel(
+    ig, full, coef, stack, ig_o, gu_o, uu_o, ge_o, ue_o, left, update_v, error_v, out_sem
+):
+    stores = [pltpu.make_async_copy(ig, ig_o, out_sem.at[4 * len(BLOCKS)])]
+    stores[0].start()
+    for p in range(2):
         value = coef[p]
         top = value.astype(BF16)
         low = (value - top.astype(F32)).astype(BF16)
-        approx = mm(jnp.concatenate([top, low, top], axis=0), stack[p], 0, 0)
-        update[...] = approx.astype(BF16)
-        error[0] = (full[p] - approx * (1.0 / (NZ * NX * NC))).astype(BF16)
+        left[p] = jnp.concatenate([top, low, top], axis=0).T
+    k = 0
+    for start, size in BLOCKS:
+        for p, (update, error) in enumerate(((gu_o, ge_o), (uu_o, ue_o))):
+            rows = pl.ds(start, size)
+            approx = mm(left[p, rows], stack[p], 1, 0)
+            update_v[p, rows] = approx.astype(BF16)
+            error_v[p, rows] = (full[p, rows] - approx * (1.0 / (NZ * NX * NC))).astype(BF16)
+            for src, dst in ((update_v, update), (error_v, error.at[0])):
+                stores.append(pltpu.make_async_copy(src.at[p, rows], dst.at[rows], out_sem.at[k]))
+                stores[-1].start()
+                k += 1
+    for store in stores:
+        store.wait()
 
 
 def on_device(tokens, hidden_grad, gate_weight, up_weight, gate_error, up_error, gate_basis, up_basis):
@@ -301,10 +313,7 @@
         main_kernel,
         name="main",
         out_shape=(
-            jax.ShapeDtypeStruct((ROWS, D), BF16),
-            jax.ShapeDtypeStruct((2, FF, D), F32),
-            jax.ShapeDtypeStruct((2, NX, CROWS, FF), F32),
-            jax.ShapeDtypeStruct((2, 3 * RANK, D), BF16),
+            V((ROWS, D), BF16), V((2, FF, D), F32), V((2, NX, CROWS, FF), F32), V((2, 3 * RANK, D), BF16),
         ),
         in_specs=[any_spec] * 8,
         out_specs=(any_spec,) * 4,
@@ -322,35 +331,39 @@
             S((8,)), S((4,)), S((copies,)), S((copies,)),
         ],
         compiler_params=pltpu.CompilerParams(
-            collective_id=0, has_side_effects=True, vmem_limit_bytes=56 << 20
+            collective_id=0, has_side_effects=True, vmem_limit_bytes=40 << 20
         ),
         cost_estimate=pl.CostEstimate(
             flops=8 * TOK * D * FF, bytes_accessed=16 << 20, transcendentals=TOK * FF
         ),
     )(
-        tokens, hidden_grad.T, gate_weight.T, up_weight.T,
-        jnp.swapaxes(gate_error, 1, 2), jnp.swapaxes(up_error, 1, 2), gate_basis, up_basis,
-    )
-    block = 128
-    out = jax.ShapeDtypeStruct((FF, D), BF16)
-    out_error = jax.ShapeDtypeStruct((1, FF, D), BF16)
-    rows = pl.BlockSpec((block, D), lambda i: (i, 0))
-    rows_error = pl.BlockSpec((1, block, D), lambda i: (0, i, 0))
-    whole = pl.BlockSpec((ROWS, D), lambda i: (0, 0))
+        *(
+            pltpu.with_memory_space_constraint(a, pltpu.HBM)
+            for a in (
+                tokens, hidden_grad.T, gate_weight.T, up_weight.T,
+                jnp.swapaxes(gate_error, 1, 2), jnp.swapaxes(up_error, 1, 2), gate_basis, up_basis,
+            )
+        )
+    )
+    out = pltpu.HBM((FF, D), BF16)
+    out_error = pltpu.HBM((1, FF, D), BF16)
     input_grad, gate_update, up_update, gate_next, up_next = pl.pallas_call(
         final_kernel,
         name="outputs",
-        grid=(pl.cdiv(FF, block),),
-        out_shape=(jax.ShapeDtypeStruct((ROWS, D), BF16), out, out, out_error, out_error),
-        in_specs=[
-            whole,
-            pl.BlockSpec((2, block, D), lambda i: (0, i, 0)),
-            pl.BlockSpec((2, RANK, block), lambda i: (0, 0, i)),
-            pl.BlockSpec((2, 3 * RANK, D), lambda i: (0, 0, 0)),
+        out_shape=(pltpu.HBM((ROWS, D), BF16), out, out, out_error, out_error),
+        in_specs=[pl.BlockSpec(memory_space=V)] * 4,
+        out_specs=(any_spec,) * 5,
+        scratch_shapes=[
+            V((2, FF, 3 * RANK), BF16), V((2, FF, D), BF16), V((2, FF, D), BF16),
+            S((4 * len(BLOCKS) + 1,)),
         ],
-        out_specs=(whole, rows, rows, rows_error, rows_error),
-        compiler_params=pltpu.CompilerParams(vmem_limit_bytes=56 << 20),
-    )(ig, full, coef.reshape(2, RANK, FF), stack)
+        compiler_params=pltpu.CompilerParams(vmem_limit_bytes=32 << 20),
+    )(
+        *(
+            pltpu.with_memory_space_constraint(a, V)
+            for a in (ig, full, coef.reshape(2, RANK, FF), stack)
+        )
+    )
     return (
         input_grad, gate_update.T, up_update.T,
         jnp.swapaxes(gate_next, 1, 2), jnp.swapaxes(up_next, 1, 2),

time: 56.1 us -> 51.9 us (0.925)
  Pallas kernels: 55.2 us -> 51.2 us
    pallas_call x2, Pallas kernels: 55.2 us -> 51.2 us  [the longest x1 48.7 us: on_device(): pl.pallas_call(main_kernel, name='main', out_shape=(V((ROWS, D), BF16), V...]
where the time goes in v2:
time: 51.9 us; the launch traced here: 51.8 us
  Pallas kernels  51.2 us (99%)
  between operations  0.64 us (1%)
    pallas_call x1, Pallas kernels, on_device(): pl.pallas_call(main_kernel, name='main', out_shape=(V((ROWS, D), BF16), V...  48.7 us
    pallas_call x1, Pallas kernels, on_device(): pl.pallas_call(final_kernel, name='outputs', out_shape=(pltpu.HBM((ROWS,...  2.48 us

profile of v2, /device:TPU:1, one launch (start us, length us, event | category | flops | bytes accessed | tf_op | source)
XLA Modules:
  0.0 51.8 jit_solution(4044218456098079334)
XLA Ops:
  0.6 48.7 %main.1 = (bf16[256,896]{1,0:T(8,128)(2,1)S(1)}, f32[2,608,896]{2,1,0:T(8,128)S(1)}, f32[2,4,8,608]{3,2,1,0:T(8,128)S(1)}, bf16[2,96,896]{2,1,0:T(8,128)(2,1)S(1)}) custom-call(bf16[1024,896]{1,0:T(8,128)(2,1)} %tok_h.1, bf16[608,1024]{1,0:T(8,128)(2,1)} %bitcast.11, bf16[608,896]{1,0:T(8,128)(2,1)} %bitcast.12, bf16[608,896]{1,0:T(8,128)(2,1)} %bitcast.13, ...), custom_call_target="tpu_custom_call" | custom-call | flops 4462739456 | bytes 16777216 | tf_op jit(solution)/shard_map/main/pallas_call | solution.py:312
  49.3 2.5 %outputs.1 = (bf16[256,896]{1,0:T(8,128)(2,1)}, bf16[608,896]{1,0:T(8,128)(2,1)}, bf16[608,896]{1,0:T(8,128)(2,1)}, bf16[1,608,896]{2,1,0:T(8,128)(2,1)}, bf16[1,608,896]{2,1,0:T(8,128)(2,1)}) custom-call(bf16[256,896]{1,0:T(8,128)(2,1)S(1)} %get-tuple-element.14.ig, f32[2,608,896]{2,1,0:T(8,128)S(1)} %get-tuple-element.15.full, f32[2,32,608]{2,1,0:T(8,128)S(1)} %bitcast.10, ...), custom_call_target="tpu_custom_call" | custom-call | tf_op jit(solution)/shard_map/outputs/pallas_call | solution.py:350

commit v3 on v2

--- a/solution.py
+++ b/solution.py
@@ -16,6 +16,9 @@
 D, FF, RANK, TOK = 896, 608, 32, 1024
 ROWS = TOK // NY
 HALF = ROWS // 2
+ORDER = (2, 1, 3, 0)
+SPLIT = 10
+PIECES = ((0, 32), (32, 96))
 SHARE = RANK // (NX * NY)
 CROWS = RANK // NX
 SCALE = 1.0 / math.sqrt(TOK)
@@ -45,10 +48,10 @@
 def main_kernel(
     tok_h, hid_h, wg_h, wu_h, eg_h, eu_h, bg_h, bu_h,
     ig_o, full_o, coef_o, stack_o,
-    tok, hid, wgt, err, basis, delta, part, half_in, whole_in, ig_b,
+    tok, hid, wgt, err, basis, delta, part, half_in,
     full, mate_full, s_high, s_low,
     f_out, f_in, f_src, f_rs, f_z, f_ag, fac, elim, h_own, h_all, stack,
-    c_src, c_rs, c_z, c_all,
+    c_src, c_rs, c_z, c_own,
     in_sem, out_sem, send_sem, recv_sem,
 ):
     dp = lax.axis_index("dp")
@@ -58,23 +61,28 @@
     z = lax.div(dp, NC * NX)
     mate = 1 - c
 
-    loads = [
-        pltpu.make_async_copy(src, dst, in_sem.at[i])
-        for i, (src, dst) in enumerate(
-            [
-                (wg_h, wgt.at[pl.ds(0, FF)]),
-                (wu_h, wgt.at[pl.ds(FF, FF)]),
-                (tok_h, tok),
-                (hid_h, hid),
-                (bg_h, basis.at[0]),
-                (bu_h, basis.at[1]),
-                (eg_h.at[0], err.at[0]),
-                (eu_h.at[0], err.at[1]),
-            ]
-        )
+    def chunk(k):
+        return pl.ds(pl.multiple_of(lax.rem(y + k, NY) * ROWS, ROWS), ROWS)
+
+    def local(k):
+        return pl.ds(k * ROWS, ROWS)
+
+    def load(src, dst):
+        copy = pltpu.make_async_copy(src, dst, in_sem.at[len(loads)])
+        copy.start()
+        loads.append(copy)
+        return copy
+
+    loads = []
+    load_first = [
+        load(wg_h, wgt.at[pl.ds(0, FF)]), load(wu_h, wgt.at[pl.ds(FF, FF)]),
     ]
-    for load in loads:
-        load.start()
+    load_chunk = {}
+    for k in ORDER:
+        load_chunk[k] = [
+            load(tok_h.at[chunk(k)], tok.at[local(k)]),
+            load(hid_h.at[:, chunk(k)], hid.at[:, local(k)]),
+        ]
 
     def at_xy(dx, dy):
         return device(z, lax.rem(x + dx, NX), c, lax.rem(y + dy, NY))
@@ -85,8 +93,15 @@
     def at_cx(dc, dx):
         return device(z, lax.rem(x + dx, NX), lax.rem(c + dc, NC), y)
 
+    def hops(*o):
+        return -sum(min(d, n - d) for d, n in o)
+
     xy = [(dx, dy) for dx in range(NX) for dy in range(NY)][1:]
+    xy.sort(key=lambda o: hops((o[0], NX), (o[1], NY)))
     cx = [(dc, dx) for dc in range(NC) for dx in range(NX)][1:]
+    cx.sort(key=lambda o: hops((o[0], NC), (o[1], NX)))
+    xs = sorted(range(1, NX), key=lambda d: hops((d, NX)))
+    zs = sorted(range(1, NZ), key=lambda d: hops((d, NZ)))
     greet = [at_xy(*o) for o in xy] + [at_z(dz) for dz in range(1, NZ)]
     greet += [at_cx(*o) for o in cx if o[0] == 1]
     barrier = pltpu.get_barrier_semaphore()
@@ -107,11 +122,8 @@
         sent.append(copy)
         return copy
 
-    for load in loads[:4]:
-        load.wait()
-
-    def act_step(i, carry):
-        cols = pl.ds(pl.multiple_of(i * ROWS, ROWS), ROWS)
+    def acts(k):
+        cols = local(k)
         act = mm(wgt[...], tok[cols, :], 1, 1)
         g, u = act[:FF], act[FF:]
         h = hid[:, cols].astype(F32)
@@ -119,12 +131,49 @@
         hs = h * s
         delta[:FF, cols] = (hs * u * (1.0 + g * (1.0 - s))).astype(BF16)
         delta[FF:, cols] = (hs * g).astype(BF16)
-        return carry
-
-    with jax.named_scope("acts"):
-        lax.fori_loop(0, NY, act_step, 0)
-    for load in loads[4:]:
-        load.wait()
+
+    def partial(k):
+        part[k] = mm(delta[:, local(k)], wgt[...], 0, 0)
+
+    load_rest = [
+        load(bg_h, basis.at[0]), load(bu_h, basis.at[1]),
+        load(eg_h.at[0], err.at[0]), load(eu_h.at[0], err.at[1]),
+    ]
+    for copy in load_first:
+        copy.wait()
+    for k in ORDER:
+        for copy in load_chunk[k]:
+            copy.wait()
+    acts(2)
+    acts(1)
+    acts(3)
+    acts(0)
+
+    up, down = at_xy(0, 1), at_xy(0, NY - 1)
+    far_up, far_down, near_up, near_down = [], [], [], []
+
+    def far(start, size):
+        at, also = pl.ds(start, size), pl.ds(HALF + start, size)
+        far_up.append(send(part.at[2, at], half_in.at[0, at], up))
+        far_down.append(send(part.at[2, also], half_in.at[1, at], down))
+
+    def near_first(start, size):
+        at, also = pl.ds(start, size), pl.ds(HALF + start, size)
+        near_up.append(send(part.at[1, also], ig_o.at[1, also], up))
+        near_down.append(send(part.at[3, at], ig_o.at[2, at], down))
+
+    def near_last(i):
+        start, size = PIECES[i]
+        at, also = pl.ds(start, size), pl.ds(HALF + start, size)
+        far_up[i].wait_recv()
+        part[1, at] = part[1, at] + half_in[0, at]
+        near_up.append(send(part.at[1, at], ig_o.at[1, at], up))
+        far_down[i].wait_recv()
+        part[3, also] = part[3, also] + half_in[1, at]
+        near_down.append(send(part.at[3, also], ig_o.at[2, also], down))
+
+    for copy in load_rest:
+        copy.wait()
 
     def pick(p):
         return pl.ds(pl.multiple_of(p * FF, FF), FF)
@@ -135,8 +184,10 @@
         e = fold(mm(b, err[p], 1, 0))
         return fold(mm(split_rows(t), tok[...], 1, 0)) * SCALE + e
 
+    partial(2)
+    pl.semaphore_wait(barrier, len(greet))
+    far(*PIECES[0])
     f_out[...] = factor_of(mate)
-    pl.semaphore_wait(barrier, len(greet))
     ex_f = send(f_out, f_in, at_cx(1, 0))
     own = factor_of(c)
     ex_f.wait_recv()
@@ -148,16 +199,14 @@
         to = lax.rem(x + dx, NX) * NY + lax.rem(y + dy, NY)
         rs.append(send(f_src.at[to], f_rs.at[i], at_xy(dx, dy)))
 
-    def partial(k):
-        cols = pl.ds(pl.multiple_of(lax.rem(y + k, NY) * ROWS, ROWS), ROWS)
-        part[k] = mm(delta[:, cols], wgt[...], 0, 0)
-
-    low, high = pl.ds(0, HALF), pl.ds(HALF, HALF)
-    partial(2)
-    far_up = send(part.at[2, low], half_in.at[0], at_xy(0, 1))
-    far_down = send(part.at[2, high], half_in.at[1], at_xy(0, NY - 1))
+    far(*PIECES[1])
+
+    def grad_of(p):
+        full[p] = mm(delta[pick(p), :], tok[...], 1, 0) * SCALE + err[p].astype(F32)
+
+    grad_of(mate)
+    ex_s = send(full.at[mate], mate_full, at_cx(1, 0))
     partial(1)
-    partial(3)
 
     mine = x * NY + y
     total = f_src[mine]
@@ -166,16 +215,12 @@
     for i in range(len(xy)):
         total = total + f_rs[i]
     f_z[z] = total
-    zs = [send(f_z.at[z], f_z.at[z], at_z(dz)) for dz in range(1, NZ)]
-
-    def grad_of(p):
-        full[p] = mm(delta[pick(p), :], tok[...], 1, 0) * SCALE + err[p].astype(F32)
-
-    grad_of(mate)
-    ex_s = send(full.at[mate], mate_full, at_cx(1, 0))
+    fz = [send(f_z.at[z], f_z.at[z], at_z(dz)) for dz in zs]
+
+    partial(3)
+    near_first(0, 32)
     grad_of(c)
-
-    for copy in zs:
+    for copy in fz:
         copy.wait_recv()
     total = f_z[0]
     for i in range(1, NZ):
@@ -183,19 +228,12 @@
     f_ag[mine] = total
     ag = [send(f_ag.at[mine], f_ag.at[mine], at_xy(dx, dy)) for dx, dy in xy]
 
-    near_up = [send(part.at[1, high], whole_in.at[0, high], at_xy(0, 1))]
-    near_down = [send(part.at[3, low], whole_in.at[1, low], at_xy(0, NY - 1))]
-    far_up.wait_recv()
-    part[1, low] = part[1, low] + half_in[0]
-    near_up.append(send(part.at[1, low], whole_in.at[0, low], at_xy(0, 1)))
-    far_down.wait_recv()
-    part[3, high] = part[3, high] + half_in[1]
-    near_down.append(send(part.at[3, high], whole_in.at[1, high], at_xy(0, NY - 1)))
+    near_first(32, 96)
 
     stores = [
         pltpu.make_async_copy(full, full_o, out_sem.at[0]),
-        pltpu.make_async_copy(ig_b, ig_o, out_sem.at[1]),
-        pltpu.make_async_copy(c_all, coef_o, out_sem.at[2]),
+        pltpu.make_async_copy(part.at[0], ig_o.at[0], out_sem.at[1]),
+        pltpu.make_async_copy(c_own, coef_o.at[c, x], out_sem.at[2]),
         pltpu.make_async_copy(stack, stack_o, out_sem.at[3]),
     ]
     stores[0].start()
@@ -204,7 +242,6 @@
     top = both.astype(BF16)
     s_high[...] = top
     s_low[...] = (both - top.astype(F32)).astype(BF16)
-    partial(0)
 
     for copy in ag:
         copy.wait_recv()
@@ -216,9 +253,11 @@
     for j in range(NX):
         c_src[j] = coef[j * CROWS:(j + 1) * CROWS]
     crs = [
-        send(c_src.at[lax.rem(x + dx, NX)], c_rs.at[x], at_cx(0, dx)) for dx in range(1, NX)
+        send(c_src.at[lax.rem(x + dx, NX)], c_rs.at[x], at_cx(0, dx)) for dx in xs
     ]
     c_rs[x] = c_src[x]
+    for i in range(len(PIECES)):
+        near_last(i)
 
     sub = lax.broadcasted_iota(jnp.int32, (RANK, 2 * RANK), 0)
     lane = lax.broadcasted_iota(jnp.int32, (RANK, 2 * RANK), 1)
@@ -232,16 +271,16 @@
         pivot = jnp.sum(jnp.where(lane[:1] == k, row, 0.0), axis=1, keepdims=True)
         return a - jnp.where(sub > k, (column / pivot) * row, 0.0)
 
-    state = lax.fori_loop(0, RANK // 2, eliminate, elim[...])
+    state = lax.fori_loop(0, SPLIT, eliminate, elim[...])
     for copy in crs:
         copy.wait_recv()
     total = c_rs[0]
     for i in range(1, NX):
         total = total + c_rs[i]
     c_z[z] = total
-    czs = [send(c_z.at[z], c_z.at[z], at_z(dz)) for dz in range(1, NZ)]
-
-    state = lax.fori_loop(RANK // 2, RANK, eliminate, state)
+    czs = [send(c_z.at[z], c_z.at[z], at_z(dz)) for dz in zs]
+
+    state = lax.fori_loop(SPLIT, RANK, eliminate, state)
     left, inverse = state[:, :RANK], state[:, RANK:]
     pivots = jnp.sum(
         jnp.where(sub[:, :RANK] == lane[:, :RANK], left, 0.0), axis=1, keepdims=True
@@ -256,9 +295,12 @@
     total = c_z[0]
     for i in range(1, NZ):
         total = total + c_z[i]
-    c_all[c, x] = total
-    cag = [send(c_all.at[c, x], c_all.at[c, x], at_cx(dc, dx)) for dc, dx in cx]
-
+    c_own[...] = total
+    cag = [send(c_own, coef_o.at[c, x], at_cx(dc, dx)) for dc, dx in cx]
+    stores[2].start()
+
+    partial(0)
+    stores[1].start()
     ex_h.wait_recv()
     for p, value in ((c, h_own[...]), (mate, h_all[...])):
         top = value.astype(BF16)
@@ -269,11 +311,8 @@
 
     for copy in near_up + near_down:
         copy.wait_recv()
-    ig_b[...] = (part[0] + (whole_in[0] + whole_in[1])).astype(BF16)
-    stores[1].start()
     for copy in cag:
         copy.wait_recv()
-    stores[2].start()
     for copy in sent:
         copy.wait_send()
     for store in stores:
@@ -281,10 +320,9 @@
 
 
 def final_kernel(
-    ig, full, coef, stack, ig_o, gu_o, uu_o, ge_o, ue_o, left, update_v, error_v, out_sem
+    ig, full, coef, stack, ig_o, gu_o, uu_o, ge_o, ue_o, left, ig_v, update_v, error_v, out_sem
 ):
-    stores = [pltpu.make_async_copy(ig, ig_o, out_sem.at[4 * len(BLOCKS)])]
-    stores[0].start()
+    stores = []
     for p in range(2):
         value = coef[p]
         top = value.astype(BF16)
@@ -301,6 +339,9 @@
                 stores.append(pltpu.make_async_copy(src.at[p, rows], dst.at[rows], out_sem.at[k]))
                 stores[-1].start()
                 k += 1
+    ig_v[...] = (ig[0] + (ig[1] + ig[2])).astype(BF16)
+    stores.append(pltpu.make_async_copy(ig_v, ig_o, out_sem.at[k]))
+    stores[-1].start()
     for store in stores:
         store.wait()
 
@@ -308,27 +349,27 @@
 def on_device(tokens, hidden_grad, gate_weight, up_weight, gate_error, up_error, gate_basis, up_basis):
     V, S = pltpu.VMEM, pltpu.SemaphoreType.DMA
     any_spec = pl.BlockSpec(memory_space=pl.ANY)
-    copies = 80
+    copies = 96
     ig, full, coef, stack = pl.pallas_call(
         main_kernel,
         name="main",
         out_shape=(
-            V((ROWS, D), BF16), V((2, FF, D), F32), V((2, NX, CROWS, FF), F32), V((2, 3 * RANK, D), BF16),
+            V((3, ROWS, D), F32), V((2, FF, D), F32), V((2, NX, CROWS, FF), F32), V((2, 3 * RANK, D), BF16),
         ),
         in_specs=[any_spec] * 8,
         out_specs=(any_spec,) * 4,
         scratch_shapes=[
             V((TOK, D), BF16), V((FF, TOK), BF16), V((2 * FF, D), BF16),
             V((2, FF, D), BF16), V((2, RANK, FF), F32), V((2 * FF, TOK), BF16),
-            V((NY, ROWS, D), F32), V((2, HALF, D), F32), V((2, ROWS, D), F32), V((ROWS, D), BF16),
+            V((NY, ROWS, D), F32), V((2, HALF, D), F32),
             V((2, FF, D), F32), V((FF, D), F32), V((D, FF), BF16), V((D, FF), BF16),
             V((RANK, D), F32), V((RANK, D), F32), V((NX * NY, SHARE, D), F32),
             V((NX * NY - 1, SHARE, D), F32), V((NZ, SHARE, D), F32), V((NX * NY, SHARE, D), F32),
             V((RANK, D), F32), V((RANK, 2 * RANK), F32), V((RANK, D), F32), V((RANK, D), F32),
             V((2, 3 * RANK, D), BF16),
             V((NX, CROWS, FF), F32), V((NX, CROWS, FF), F32), V((NZ, CROWS, FF), F32),
-            V((2, NX, CROWS, FF), F32),
-            S((8,)), S((4,)), S((copies,)), S((copies,)),
+            V((CROWS, FF), F32),
+            S((18,)), S((4,)), S((copies,)), S((copies,)),
         ],
         compiler_params=pltpu.CompilerParams(
             collective_id=0, has_side_effects=True, vmem_limit_bytes=40 << 20
@@ -354,7 +395,8 @@
         in_specs=[pl.BlockSpec(memory_space=V)] * 4,
         out_specs=(any_spec,) * 5,
         scratch_shapes=[
-            V((2, FF, 3 * RANK), BF16), V((2, FF, D), BF16), V((2, FF, D), BF16),
+            V((2, FF, 3 * RANK), BF16), V((ROWS, D), BF16),
+            V((2, FF, D), BF16), V((2, FF, D), BF16),
             S((4 * len(BLOCKS) + 1,)),
         ],
         compiler_params=pltpu.CompilerParams(vmem_limit_bytes=32 << 20),

time: 51.9 us -> 50.2 us (0.967)
  Pallas kernels: 51.2 us -> 49.3 us
    pallas_call x1, Pallas kernels: 48.7 us -> 46.7 us  [on_device(): pl.pallas_call(main_kernel, name='main', out_shape=(V((3, ROWS, D), F32),...]
where the time goes in v3:
time: 50.2 us; the launch traced here: 50.1 us
  Pallas kernels  49.3 us (98%)
  between operations  0.8 us (2%)
    pallas_call x1, Pallas kernels, on_device(): pl.pallas_call(main_kernel, name='main', out_shape=(V((3, ROWS, D), F32),...  46.7 us
    pallas_call x1, Pallas kernels, on_device(): pl.pallas_call(final_kernel, name='outputs', out_shape=(pltpu.HBM((ROWS,...  2.64 us

profile of v3, /device:TPU:1, one launch (start us, length us, event | category | flops | bytes accessed | tf_op | source)
XLA Modules:
  0.0 50.1 jit_solution(3872174710911755240)
XLA Ops:
  0.6 46.7 %main.1 = (f32[3,256,896]{2,1,0:T(8,128)S(1)}, f32[2,608,896]{2,1,0:T(8,128)S(1)}, f32[2,4,8,608]{3,2,1,0:T(8,128)S(1)}, bf16[2,96,896]{2,1,0:T(8,128)(2,1)S(1)}) custom-call(bf16[1024,896]{1,0:T(8,128)(2,1)} %tok_h.1, bf16[608,1024]{1,0:T(8,128)(2,1)} %bitcast.11, bf16[608,896]{1,0:T(8,128)(2,1)} %bitcast.12, bf16[608,896]{1,0:T(8,128)(2,1)} %bitcast.13, ...), custom_call_target="tpu_custom_call" | custom-call | flops 4462739456 | bytes 16777216 | tf_op jit(solution)/shard_map/main/pallas_call | solution.py:353
  47.3 2.6 %outputs.1 = (bf16[256,896]{1,0:T(8,128)(2,1)}, bf16[608,896]{1,0:T(8,128)(2,1)}, bf16[608,896]{1,0:T(8,128)(2,1)}, bf16[1,608,896]{2,1,0:T(8,128)(2,1)}, bf16[1,608,896]{2,1,0:T(8,128)(2,1)}) custom-call(f32[3,256,896]{2,1,0:T(8,128)S(1)} %get-tuple-element.14.ig, f32[2,608,896]{2,1,0:T(8,128)S(1)} %get-tuple-element.15.full, f32[2,32,608]{2,1,0:T(8,128)S(1)} %bitcast.10, ...), custom_call_target="tpu_custom_call" | custom-call | tf_op jit(solution)/shard_map/outputs/pallas_call | solution.py:391

commit v4 on v3

--- a/solution.py
+++ b/solution.py
@@ -243,6 +243,7 @@
     s_high[...] = top
     s_low[...] = (both - top.astype(F32)).astype(BF16)
 
+    near_last(0)
     for copy in ag:
         copy.wait_recv()
     for s in range(NX * NY):
@@ -256,8 +257,7 @@
         send(c_src.at[lax.rem(x + dx, NX)], c_rs.at[x], at_cx(0, dx)) for dx in xs
     ]
     c_rs[x] = c_src[x]
-    for i in range(len(PIECES)):
-        near_last(i)
+    near_last(1)
 
     sub = lax.broadcasted_iota(jnp.int32, (RANK, 2 * RANK), 0)
     lane = lax.broadcasted_iota(jnp.int32, (RANK, 2 * RANK), 1)

time: 50.2 us -> 50.2 us (level)
  no operation moved by 1% of the time
where the time goes in v4:
time: 50.2 us; the launch traced here: 50.1 us
  Pallas kernels  49.3 us (98%)
  between operations  0.8 us (2%)
    pallas_call x1, Pallas kernels, on_device(): pl.pallas_call(main_kernel, name='main', out_shape=(V((3, ROWS, D), F32),...  46.7 us
    pallas_call x1, Pallas kernels, on_device(): pl.pallas_call(final_kernel, name='outputs', out_shape=(pltpu.HBM((ROWS,...  2.64 us

profile of v4, /device:TPU:1, one launch (start us, length us, event | category | flops | bytes accessed | tf_op | source)
XLA Modules:
  0.0 50.1 jit_solution(9718076260330377039)
XLA Ops:
  0.6 46.7 %main.1 = (f32[3,256,896]{2,1,0:T(8,128)S(1)}, f32[2,608,896]{2,1,0:T(8,128)S(1)}, f32[2,4,8,608]{3,2,1,0:T(8,128)S(1)}, bf16[2,96,896]{2,1,0:T(8,128)(2,1)S(1)}) custom-call(bf16[1024,896]{1,0:T(8,128)(2,1)} %tok_h.1, bf16[608,1024]{1,0:T(8,128)(2,1)} %bitcast.11, bf16[608,896]{1,0:T(8,128)(2,1)} %bitcast.12, bf16[608,896]{1,0:T(8,128)(2,1)} %bitcast.13, ...), custom_call_target="tpu_custom_call" | custom-call | flops 4462739456 | bytes 16777216 | tf_op jit(solution)/shard_map/main/pallas_call | solution.py:353
  47.3 2.6 %outputs.1 = (bf16[256,896]{1,0:T(8,128)(2,1)}, bf16[608,896]{1,0:T(8,128)(2,1)}, bf16[608,896]{1,0:T(8,128)(2,1)}, bf16[1,608,896]{2,1,0:T(8,128)(2,1)}, bf16[1,608,896]{2,1,0:T(8,128)(2,1)}) custom-call(f32[3,256,896]{2,1,0:T(8,128)S(1)} %get-tuple-element.14.ig, f32[2,608,896]{2,1,0:T(8,128)S(1)} %get-tuple-element.15.full, f32[2,32,608]{2,1,0:T(8,128)S(1)} %bitcast.10, ...), custom_call_target="tpu_custom_call" | custom-call | tf_op jit(solution)/shard_map/outputs/pallas_call | solution.py:391
